TPU v7x, 128 devices: a whole 4x4x4 slice. The times are simulated.
128 devices in a mesh: seq: 8 (over x, core), head: 16 (over z, y).
Axes of the slice: x: 4, y: 4, z: 4, core: 2. Of those that a mesh axis runs over, the one named last changes fastest.
Arguments:
- tokens: bfloat16 [1024, 6144], P('seq'), may hold values from -6 to 6
- log_decay: float32 [1024, 32], P('seq', 'head'), may hold values from -1 to 0
- carried_state: float32 [32, 128, 128], P('head'), may hold values from -48 to 48
- q_weight: bfloat16 [6144, 4096], P(None, 'head'), may hold values from -0.078125 to 0.078125
- k_weight: bfloat16 [6144, 4096], P(None, 'head'), may hold values from -0.078125 to 0.078125
- v_weight: bfloat16 [6144, 4096], P(None, 'head'), may hold values from -0.078125 to 0.078125
- out_weight: bfloat16 [4096, 6144], P('head'), may hold values from -0.09375 to 0.09375
- final_gain: bfloat16 [6144], replicated, may hold values from 0.099609375 to 1.8984375
- vocab_weight: bfloat16 [6144, 131072], P(None, ('seq', 'head')), may hold values from -5 to 5
- targets: int32 [1024], replicated, may hold values from 0 to 131071
Outputs:
- loglik: float32 [1024], P('seq')
All inputs are finite; a program needn't handle non-finite values.
Results may differ from a plain program's by a relative error of at most 0.002.
Values may be sent and summed in bfloat16 or wider, within the bound.
No kernel may reach another device: no remote copies, remote signals or barrier semaphores. Data moves between devices by JAX's collectives and lax.ppermute only.
A program may use at most 128 MiB of HBM per device.

v0:
```python
import jax
import jax.numpy as jnp
from jax import lax
from jax.sharding import PartitionSpec as P


def prefix(array, axis, combine, identity):
    length, here = (lax.axis_size(axis), lax.axis_index(axis))
    everything = jax.tree.map(lambda part: lax.all_gather(part, axis), array)
    start = jax.tree.map(
        lambda part, zero: jnp.broadcast_to(jnp.asarray(zero, part.dtype), part.shape),
        array,
        identity,
    )

    def turn(k, before):
        reached = k < here
        new = combine(before, jax.tree.map(lambda part: part[k], everything))
        return jax.tree.map(lambda a, b: jnp.where(reached, a, b), new, before)

    return lax.fori_loop(0, length, turn, start)


def combine_states(earlier, later):
    return (earlier[0] * later[0], later[0][:, None, None] * earlier[1] + later[1])


def shards(
    tokens,
    log_decay,
    carried_state,
    q_weight,
    k_weight,
    v_weight,
    out_weight,
    final_gain,
    vocab_weight,
    targets,
):
    highest = lax.Precision.HIGHEST
    rows_here = tokens.shape[0]
    heads_here = carried_state.shape[0]
    head_size = carried_state.shape[1]
    view = (rows_here, heads_here, head_size)
    queries = (
        jnp.dot(tokens, q_weight, preferred_element_type=jnp.float32)
        .astype(jnp.bfloat16)
        .reshape(view)
    )
    keys_loc = (
        jnp.dot(tokens, k_weight, preferred_element_type=jnp.float32)
        .astype(jnp.bfloat16)
        .reshape(view)
    )
    values = (
        jnp.dot(tokens, v_weight, preferred_element_type=jnp.float32)
        .astype(jnp.bfloat16)
        .reshape(view)
    )
    cumul = jnp.cumsum(log_decay, axis=0)
    last_cum = cumul[-1]
    ends = jnp.exp(last_cum[None, :] - cumul)
    local_state = jnp.einsum(
        "thd,the->hde",
        keys_loc.astype(jnp.float32) * ends[:, :, None],
        values.astype(jnp.float32),
        precision=highest,
    )
    total_decay = jnp.exp(last_cum)
    prefix_decay, prefix_state = prefix(
        (total_decay, local_state),
        "seq",
        combine_states,
        (jnp.ones_like(total_decay), jnp.zeros_like(local_state)),
    )
    lower = jnp.arange(rows_here)[:, None] >= jnp.arange(rows_here)[None, :]
    scores = jnp.einsum("thd,shd->hts", queries, keys_loc, preferred_element_type=jnp.float32)
    diff = jnp.transpose(cumul[:, None, :] - cumul[None, :, :], (2, 0, 1))
    weight = (scores * jnp.exp(jnp.where(lower[None], diff, -1e30))).astype(jnp.bfloat16)
    intra = jnp.einsum("hts,shd->thd", weight, values, preferred_element_type=jnp.float32)
    state_in = prefix_decay[:, None, None] * carried_state + prefix_state
    inter = jnp.exp(cumul)[:, :, None] * jnp.einsum(
        "thd,hde->the", queries.astype(jnp.float32), state_in, precision=highest
    )
    attended = intra + inter
    normed_heads = attended * lax.rsqrt(
        jnp.mean(attended * attended, axis=-1, keepdims=True) + 1e-06
    )
    flat_heads = normed_heads.astype(jnp.bfloat16).reshape(rows_here, heads_here * head_size)
    rows_mine = rows_here // lax.axis_size("head")
    head_index = lax.axis_index("head")
    mixed_all = lax.psum(
        jnp.dot(flat_heads, out_weight, preferred_element_type=jnp.float32), "head"
    )
    mixed = lax.dynamic_slice_in_dim(mixed_all, head_index * rows_mine, rows_mine, 0)
    resid = (
        lax.dynamic_slice_in_dim(tokens, head_index * rows_mine, rows_mine, 0).astype(jnp.float32)
        + mixed
    )
    final_rows = (
        resid
        * lax.rsqrt(jnp.mean(resid * resid, axis=-1, keepdims=True) + 1e-06)
        * final_gain.astype(jnp.float32)
    )
    final_rows = final_rows.astype(jnp.bfloat16)
    vocab_local = vocab_weight.shape[1]
    offset = (lax.axis_index("seq") * lax.axis_size("head") + head_index) * vocab_local
    columns = jnp.arange(vocab_local, dtype=jnp.int32)
    logits = jnp.dot(
        lax.all_gather(final_rows, ("seq", "head"), axis=0, tiled=True),
        vocab_weight,
        preferred_element_type=jnp.float32,
    )
    top = jnp.max(logits, axis=1)
    total = jnp.sum(jnp.exp(logits - top[:, None]), axis=1)
    wanted = targets - offset
    hit = jnp.sum(jnp.where(columns[None, :] == wanted[:, None], logits, 0.0), axis=1)
    top_all = lax.pmax(top, ("seq", "head"))
    total_all, hit_all = lax.psum((total * jnp.exp(top - top_all), hit), ("seq", "head"))
    loglik = hit_all - top_all - jnp.log(total_all)
    return lax.dynamic_slice_in_dim(loglik, lax.axis_index("seq") * rows_here, rows_here, 0)


def solution(mesh):
    return jax.shard_map(
        shards,
        mesh=mesh,
        in_specs=(
            P("seq", None),
            P("seq", "head"),
            P("head", None, None),
            P(None, "head"),
            P(None, "head"),
            P(None, "head"),
            P("head", None),
            P(),
            P(None, ("seq", "head")),
            P(),
        ),
        out_specs=P("seq"),
        check_vma=False,
    )
```

profile of v0, /device:TPU:1, one launch (start us, length us, event | category | flops | bytes accessed | tf_op | source)
XLA Modules:
  0.0 385.3 jit_solution(14718534888018662489)
XLA Ops:
  6.5 0.0 copy-start
  6.5 0.0 all-gather.7.cloned.1.call-start
  6.5 0.9 copy.23
  7.5 0.2 reduce_window_sum.11
  7.7 0.1 copy.30
  7.7 3.0 convolution_convert_fusion
  10.7 0.1 copy.36
  10.8 3.0 fusion.4
  13.8 0.9 fusion.8
  14.6 0.0 all-gather.7.cloned.1.call-update
  14.7 0.0 all-reduce.3.cloned.1.call-start
  14.7 11.8 %all-gather.1 = f32[8,1,2]{2,1,0:T(1,128)S(1)} all-gather(f32[1,1,2]{2,1,0:T(1,128)S(1)} %get-tuple-element.171), channel_id=1, replica_groups=mesh['seq'=8,'head'=16] {'seq'}, dimensions={0}, use_global_device_ids=true | all-gather | bytes 72 | tf_op jit(solution)/shard_map/all_gather | solution.py:9
  26.5 0.1 copy.27
  26.6 0.1 copy.24
  26.7 3.1 fusion.5
  29.8 12.0 %all-gather.7.cloned.1.call-done = f32[16,128,128]{2,1,0:T(8,128)} async-done(((f32[2,128,128]{2,1,0:T(8,128)}), f32[16,128,128]{2,1,0:T(8,128)}) %all-gather.7.cloned.1.call-update) | async-done | bytes 1048592 | tf_op jit(solution)/shard_map/all_gather | solution.py:9
  41.8 8.3 %while.16 = (s32[]{:T(128)}, f32[2]{0:T(128)S(1)}, f32[2,128,128]{2,1,0:T(8,128)S(1)}, s32[]{:T(128)}, f32[8,2]{1,0:T(8,128)S(1)}, /*index=5*/f32[8,2,128,128]{3,2,1,0:T(8,128)}, s32[]{:T(128)}, s32[]{:T(128)}) while((s32[]{:T(128)}, f32[2]{0:T(128)S(1)}, f32[2,128,128]{2,1,0:T(8,128)S(1)}, s32[]{:T(128)}, f32[8,2]{1,0:T(8,128)S(1)}, ...), condition=%wide.region_2.3_spmd.clone, body=%wide.region_1.2_spmd.clone.sunk | while | flops 131082 | bytes 393371 | solution.py:21
  41.8 1.0 fusion.48
  42.8 1.0 fusion.48
  43.9 1.0 fusion.48
  44.9 1.0 fusion.48
  46.0 1.0 fusion.48
  47.0 1.0 fusion.48
  48.0 1.0 fusion.48
  49.1 1.0 fusion.48
  50.1 1.9 fusion.1
  52.0 1.2 multiply_reduce_fusion.1
  53.3 0.0 copy-done
  53.3 2.3 fusion.35
  55.6 0.0 copy-start.1
  55.6 0.0 copy-start.2
  55.6 0.0 all-reduce.3.cloned.1.call-update
  55.6 0.0 all-gather.5.cloned.1.call-start
  55.7 0.6 copy-done.1
  56.3 94.3 %all-reduce.3.cloned.1.call-done = f32[128,6144]{1,0:T(8,128)} async-done(((f32[128,6144]{1,0:T(8,128)}), f32[128,6144]{1,0:T(8,128)}) %all-reduce.3.cloned.1.call-update) | async-done | bytes 3145744 | tf_op jit(solution)/shard_map/psum | solution.py:92
  150.6 1.2 multiply_reduce_fusion
  151.8 1.7 multiply_convert_fusion
  153.5 0.0 all-gather.5.cloned.1.call-update
  153.5 0.0 copy-done.2
  153.6 73.3 %all-gather.5.cloned.1.call-done = bf16[1024,6144]{1,0:T(8,128)(2,1)} async-done(((bf16[8,6144]{1,0:T(8,128)(2,1)}), bf16[1024,6144]{1,0:T(8,128)(2,1)}) %all-gather.5.cloned.1.call-update) | async-done | bytes 12582928 | tf_op jit(solution)/shard_map/all_gather | solution.py:110
  226.9 19.4 %fusion.34 = (f32[1024]{0:T(1024)S(1)}, f32[1024,1024]{0,1:T(8,128)}) fusion(bf16[1024,6144]{1,0:T(8,128)(2,1)} %all-gather.5.cloned.1.call-done, bf16[6144,1024]{1,0:T(8,128)(2,1)} %param.20), kind=kOutput, calls=%fused_computation.57 | convolution fusion | flops 12885949440 | bytes 29364224 | tf_op jit(solution)/shard_map/dot_general | solution.py:109
  246.3 64.4 %pmax.7 = f32[1024]{0:T(1024)S(1)} all-reduce(f32[1024]{0:T(1024)S(1)} %get-tuple-element.174), channel_id=1, replica_groups=mesh['seq'=8,'head'=16] {'seq','head'}, use_global_device_ids=true, to_apply=%region_9.10 | all-reduce | flops 1024 | bytes 8192 | tf_op jit(solution)/shard_map/pmax | solution.py:118
  310.7 3.3 select_reduce_fusion
  314.0 64.2 %all-reduce = (f32[1024]{0:T(1024)S(1)}, f32[1024]{0:T(1024)S(1)}) all-reduce(f32[1024]{0:T(1024)S(1)} %exponential_multiply_fusion, f32[1024]{0:T(1024)S(1)} %get-tuple-element.150), channel_id=1, replica_groups=mesh['seq'=8,'head'=16] {'seq','head'}, use_global_device_ids=true, to_apply=%region_11.12 | all-reduce | flops 2048 | bytes 16384 | tf_op jit(solution)/shard_map/psum | solution.py:119
  378.2 0.6 dynamic_slice.25
  (20 shorter events, 0.3 us)
Async XLA Ops:
  6.5 46.7 %copy-start = (bf16[256,6144]{1,0:T(8,128)(2,1)S(1)}, bf16[256,6144]{1,0:T(8,128)(2,1)}, u32[]{:S(2)}) copy-start(bf16[256,6144]{1,0:T(8,128)(2,1)} %param.18) | copy-start | bytes 9437188
  6.5 35.2 %all-gather.7.cloned.1.call-start = ((), (), s32[]{:S(2)}) async-start(), calls=%async_computation.2 | async-start | bytes 1179648 | tf_op jit(solution)/shard_map/all_gather | solution.py:9
  14.7 135.9 %all-reduce.3.cloned.1.call-start = ((), (), s32[]{:S(2)}) async-start(), calls=%async_computation | async-start | bytes 6291456 | tf_op jit(solution)/shard_map/psum | solution.py:92
  55.6 0.7 copy-start.1
  55.6 98.0 %copy-start.2 = (s32[1024]{0:T(1024)S(1)}, s32[1024]{0:T(1024)}, u32[]{:S(2)}) copy-start(s32[1024]{0:T(1024)} %param.21) | copy-start | bytes 12292
  55.6 171.3 %all-gather.5.cloned.1.call-start = ((), (), s32[]{:S(2)}) async-start(), calls=%async_computation.1 | async-start | bytes 12681216 | tf_op jit(solution)/shard_map/all_gather | solution.py:110
Sparse Core Ops, SparseCore 0:
  14.8 26.9 all-gather.6
  55.7 94.8 all-reduce.2
  153.7 73.0 all-gather.4
where the time goes:
time: 386 us; the launch traced here: 385 us
  waiting for transfers between devices  180 us (47%)
  blocking collectives  140 us (36%)
  matrix products  34.7 us (9%)
  other arithmetic  14.5 us (4%)
  between operations  13.2 us (3%)
    psum x1, waiting for transfers between devices, shards(): lax.psum(jnp.dot(flat_heads, out_weight, preferred_element_type=jnp.float...  94.3 us
    all_gather x1, waiting for transfers between devices, shards(): lax.all_gather(final_rows, ('seq', 'head'), axis=0, tiled=True)  73.3 us
    pmax x1, blocking collectives, shards(): top_all = lax.pmax(top, ('seq', 'head'))  64.4 us
    psum x1, blocking collectives, shards(): lax.psum((total * jnp.exp(top - top_all), hit), ('seq', 'head'))  64.2 us
    dot_general x1, matrix products, shards(): jnp.dot(lax.all_gather(final_rows, ('seq', 'head'), axis=0, tiled=True),...  19.4 us
    all_gather x1, waiting for transfers between devices, prefix(): everything = jax.tree.map(lambda part: lax.all_gather(part, axis), array)  12 us
    all_gather x1, blocking collectives, prefix(): everything = jax.tree.map(lambda part: lax.all_gather(part, axis), array)  11.8 us
    select_n x16, other arithmetic, turn(): return jax.tree.map(lambda a, b: jnp.where(reached, a, b), new, before)  8.09 us
  transfers between devices with their start and end apart: 3, of which 3 were waited for; matrix products, arithmetic and copies ran while one was open for 1% of the time, Pallas kernels for 0%

commit v1 on v0

--- a/solution.py
+++ b/solution.py
@@ -2,6 +2,16 @@
 import jax.numpy as jnp
 from jax import lax
 from jax.sharding import PartitionSpec as P
+
+put_members_all_over_axis = lambda packet: jnp.concatenate(
+    lax.all_to_all(
+        jnp.stack([packet for _ in range(lax.axis_size(("seq", "head")))], axis=0),
+        ("seq", "head"),
+        0,
+        0,
+    ),
+    axis=0,
+)
 
 
 def prefix(array, axis, combine, identity):
@@ -107,9 +117,7 @@
     offset = (lax.axis_index("seq") * lax.axis_size("head") + head_index) * vocab_local
     columns = jnp.arange(vocab_local, dtype=jnp.int32)
     logits = jnp.dot(
-        lax.all_gather(final_rows, ("seq", "head"), axis=0, tiled=True),
-        vocab_weight,
-        preferred_element_type=jnp.float32,
+        put_members_all_over_axis(final_rows), vocab_weight, preferred_element_type=jnp.float32
     )
     top = jnp.max(logits, axis=1)
     total = jnp.sum(jnp.exp(logits - top[:, None]), axis=1)

time: 386 us -> 483 us (1.25)
  waiting for transfers between devices: 180 us -> 261 us
  starting transfers between devices: 0.09 us -> 8.1 us
  local copies, waits for them, and re-layouts: 2.47 us -> 8.56 us
    all_to_all x0 -> x1, waiting for transfers between devices: none -> 154 us  [lax.all_to_all(jnp.stack([packet for _ in range(lax.axis_size(('seq', 'he...]
    all_gather x1 -> x0, waiting for transfers between devices: 73.3 us -> none  [shards(): lax.all_gather(final_rows, ('seq', 'head'), axis=0, tiled=True)]
    all_to_all x0 -> x1, starting transfers between devices: none -> 8.06 us  [lax.all_to_all(jnp.stack([packet for _ in range(lax.axis_size(('seq', 'he...]
    another operation x0 -> x1, local copies, waits for them, and re-layouts: none -> 6.04 us  [jnp.stack([packet for _ in range(lax.axis_size(('seq', 'head')))], axis=0)]
where the time goes in v1:
time: 483 us; the launch traced here: 482 us
  waiting for transfers between devices  261 us (54%)
  blocking collectives  143 us (30%)
  matrix products  34.7 us (7%)
  other arithmetic  13.9 us (3%)
  between operations  13.5 us (3%)
  local copies, waits for them, and re-layouts  8.56 us (2%)
  starting transfers between devices  8.1 us (2%)
    all_to_all x1, waiting for transfers between devices, lax.all_to_all(jnp.stack([packet for _ in range(lax.axis_size(('seq', 'he...  154 us
    psum x1, waiting for transfers between devices, shards(): lax.psum(jnp.dot(flat_heads, out_weight, preferred_element_type=jnp.float...  94.3 us
    pmax x1, blocking collectives, shards(): top_all = lax.pmax(top, ('seq', 'head'))  66.8 us
    psum x1, blocking collectives, shards(): lax.psum((total * jnp.exp(top - top_all), hit), ('seq', 'head'))  64.2 us
    dot_general x1, matrix products, shards(): jnp.dot(put_members_all_over_axis(final_rows), vocab_weight, preferred_el...  19.4 us
    all_gather x1, waiting for transfers between devices, prefix(): everything = jax.tree.map(lambda part: lax.all_gather(part, axis), array)  12 us
    all_gather x1, blocking collectives, prefix(): everything = jax.tree.map(lambda part: lax.all_gather(part, axis), array)  11.8 us
  transfers between devices with their start and end apart: 3, of which 3 were waited for; matrix products, arithmetic and copies ran while one was open for 1% of the time, Pallas kernels for 0%

profile of v1, /device:TPU:1, one launch (start us, length us, event | category | flops | bytes accessed | tf_op | source)
XLA Modules:
  0.0 482.5 jit_solution(2064878768983144396)
XLA Ops:
  6.5 0.0 copy-start
  6.5 0.0 all-gather.4.cloned.1.call-start
  6.5 0.9 copy.23
  7.5 0.2 reduce_window_sum.11
  7.7 0.1 copy.30
  7.7 3.0 convolution_convert_fusion
  10.7 0.1 copy.36
  10.8 3.0 fusion.6
  13.8 0.9 fusion.10
  14.6 0.0 all-gather.4.cloned.1.call-update
  14.7 0.0 all-reduce.3.cloned.1.call-start
  14.7 11.8 %all-gather.1 = f32[8,1,2]{2,1,0:T(1,128)S(1)} all-gather(f32[1,1,2]{2,1,0:T(1,128)S(1)} %get-tuple-element.171), channel_id=1, replica_groups=mesh['seq'=8,'head'=16] {'seq'}, dimensions={0}, use_global_device_ids=true | all-gather | bytes 72 | tf_op jit(solution)/shard_map/all_gather | solution.py:19
  26.5 0.1 copy.27
  26.6 0.1 copy.24
  26.7 3.1 fusion.7
  29.8 12.0 %all-gather.4.cloned.1.call-done = f32[16,128,128]{2,1,0:T(8,128)} async-done(((f32[2,128,128]{2,1,0:T(8,128)}), f32[16,128,128]{2,1,0:T(8,128)}) %all-gather.4.cloned.1.call-update) | async-done | bytes 1048592 | tf_op jit(solution)/shard_map/all_gather | solution.py:19
  41.8 8.3 %while.16 = (s32[]{:T(128)}, f32[2]{0:T(128)S(1)}, f32[2,128,128]{2,1,0:T(8,128)S(1)}, s32[]{:T(128)}, f32[8,2]{1,0:T(8,128)S(1)}, /*index=5*/f32[8,2,128,128]{3,2,1,0:T(8,128)}, s32[]{:T(128)}, s32[]{:T(128)}) while((s32[]{:T(128)}, f32[2]{0:T(128)S(1)}, f32[2,128,128]{2,1,0:T(8,128)S(1)}, s32[]{:T(128)}, f32[8,2]{1,0:T(8,128)S(1)}, ...), condition=%wide.region_2.3_spmd.clone, body=%wide.region_1.2_spmd.clone.sunk | while | flops 131082 | bytes 393371 | solution.py:31
  41.8 1.0 fusion.49
  42.8 1.0 fusion.49
  43.9 1.0 fusion.49
  44.9 1.0 fusion.49
  45.9 1.0 fusion.49
  47.0 1.0 fusion.49
  48.0 1.0 fusion.49
  49.1 1.0 fusion.49
  50.1 1.9 fusion.3
  52.0 1.2 multiply_reduce_fusion.1
  53.3 0.0 copy-done
  53.3 2.3 fusion.37
  55.6 0.0 copy-start.1
  55.6 0.0 all-reduce.3.cloned.1.call-update
  55.6 0.7 copy-done.1
  56.3 94.3 %all-reduce.3.cloned.1.call-done = f32[128,6144]{1,0:T(8,128)} async-done(((f32[128,6144]{1,0:T(8,128)}), f32[128,6144]{1,0:T(8,128)}) %all-reduce.3.cloned.1.call-update) | async-done | bytes 3145744 | tf_op jit(solution)/shard_map/psum | solution.py:102
  150.6 1.2 multiply_reduce_fusion
  151.8 1.1 multiply_convert_fusion
  152.9 6.0 %stack.2 = bf16[128,8,6144]{2,1,0:T(8,128)(2,1)} broadcast(bf16[8,6144]{1,0:T(8,128)(2,1)S(1)} %multiply_convert_fusion), dimensions={1,2} | broadcast | bytes 12681216 | tf_op jit(solution)/shard_map/stack | solution.py:8
  158.9 0.0 copy-start.2
  158.9 8.1 %all-to-all-start = ((bf16[128,8,6144]{2,1,0:T(8,128)(2,1)}), bf16[128,8,6144]{2,1,0:T(8,128)(2,1)}, u32[]{:S(2)}, u32[]{:S(2)}) async-start(bf16[128,8,6144]{2,1,0:T(8,128)(2,1)} %stack.2), calls=%async_computation | async-start | bytes 25165824 | tf_op jit(solution)/shard_map/all_to_all | solution.py:7
  167.0 0.0 copy-done.2
  167.0 154.3 %all-to-all-done = bf16[128,8,6144]{2,1,0:T(8,128)(2,1)} async-done(((bf16[128,8,6144]{2,1,0:T(8,128)(2,1)}), bf16[128,8,6144]{2,1,0:T(8,128)(2,1)}, u32[]{:S(2)}, u32[]{:S(2)}) %all-to-all-start) | async-done | bytes 12582944 | tf_op jit(solution)/shard_map/all_to_all | solution.py:7
  321.3 19.4 %fusion.36 = (f32[1024]{0:T(1024)S(1)}, f32[1024,1024]{0,1:T(8,128)}) fusion(bf16[6144,1024]{1,0:T(8,128)(2,1)} %param.20, bf16[128,8,6144]{2,1,0:T(8,128)(2,1)} %all-to-all-done), kind=kOutput, calls=%fused_computation.59 | convolution fusion | flops 12885949440 | bytes 29364224 | tf_op jit(solution)/shard_map/dot_general | solution.py:119
  340.7 66.8 %pmax.7 = f32[1024]{0:T(1024)S(1)} all-reduce(f32[1024]{0:T(1024)S(1)} %get-tuple-element.174), channel_id=1, replica_groups=mesh['seq'=8,'head'=16] {'seq','head'}, use_global_device_ids=true, to_apply=%region_9.10 | all-reduce | flops 1024 | bytes 8192 | tf_op jit(solution)/shard_map/pmax | solution.py:126
  407.5 3.3 select_reduce_fusion
  410.8 64.2 %all-reduce = (f32[1024]{0:T(1024)S(1)}, f32[1024]{0:T(1024)S(1)}) all-reduce(f32[1024]{0:T(1024)S(1)} %exponential_multiply_fusion, f32[1024]{0:T(1024)S(1)} %get-tuple-element.150), channel_id=1, replica_groups=mesh['seq'=8,'head'=16] {'seq','head'}, use_global_device_ids=true, to_apply=%region_11.12 | all-reduce | flops 2048 | bytes 16384 | tf_op jit(solution)/shard_map/psum | solution.py:127
  475.1 0.6 dynamic_slice.25
  (20 shorter events, 0.3 us)
Async XLA Ops:
  6.5 46.7 %copy-start = (bf16[256,6144]{1,0:T(8,128)(2,1)S(1)}, bf16[256,6144]{1,0:T(8,128)(2,1)}, u32[]{:S(2)}) copy-start(bf16[256,6144]{1,0:T(8,128)(2,1)} %param.18) | copy-start | bytes 9437188
  6.5 35.2 %all-gather.4.cloned.1.call-start = ((), (), s32[]{:S(2)}) async-start(), calls=%async_computation.2 | async-start | bytes 1179648 | tf_op jit(solution)/shard_map/all_gather | solution.py:19
  14.7 135.9 %all-reduce.3.cloned.1.call-start = ((), (), s32[]{:S(2)}) async-start(), calls=%async_computation.1 | async-start | bytes 6291456 | tf_op jit(solution)/shard_map/psum | solution.py:102
  55.6 0.7 copy-start.1
  158.9 8.1 %copy-start.2 = (s32[1024]{0:T(1024)S(1)}, s32[1024]{0:T(1024)}, u32[]{:S(2)}) copy-start(s32[1024]{0:T(1024)} %param.21) | copy-start | bytes 12292
  158.9 162.4 %all-to-all-start = ((bf16[128,8,6144]{2,1,0:T(8,128)(2,1)}), bf16[128,8,6144]{2,1,0:T(8,128)(2,1)}, u32[]{:S(2)}, u32[]{:S(2)}) async-start(bf16[128,8,6144]{2,1,0:T(8,128)(2,1)} %stack.2), calls=%async_computation | async-start | bytes 25165824 | tf_op jit(solution)/shard_map/all_to_all | solution.py:7
Sparse Core Ops, SparseCore 0:
  14.8 26.9 all-gather.3
  55.7 94.8 all-reduce.2
